TPU v7x, 32 devices: a whole 2x2x4 slice. The times are simulated.
32 devices in a mesh: groups: 2 (over y), dir: 2 (over x), space: 4 (over z), freq: 2 (over core).
Axes of the slice: x: 2, y: 2, z: 4, core: 2. Of those that a mesh axis runs over, the one named last changes fastest.
Arguments:
- spectrum: float32 [36, 32, 192, 256], P('dir', 'freq', ('groups', 'space')), parts along dimension 2, may hold values from 0.05 to 2
- land_mask: int32 [192, 256], P(('groups', 'space')), parts along dimension 0, may hold values 0 or 1
- depth_class: int32 [192, 256], P(('groups', 'space')), parts along dimension 0, may hold values from 0 to 7
- shift_count: int32 [192, 8], P(('groups', 'space')), parts along dimension 0, may hold values from -2 to 2
- turning: float32 [192, 256], P(('groups', 'space')), parts along dimension 0, may hold values from 0 to 1
- wind_rate: float32 [192, 256], P(('groups', 'space')), parts along dimension 0, may hold values from 0.02 to 0.2
- wind_angle: float32 [192, 256], P(('groups', 'space')), parts along dimension 0, may hold values from -3.140625 to 3.140625
- cfl: float32 [32], replicated, may hold values from 0.3 to 0.7
- freq_turn: float32 [32], replicated, may hold values from 0.3 to 1
- friction_table: float32 [8, 32], replicated, may hold values from 0.02 to 0.3
- transfer: float32 [1152, 1152], replicated, may hold values from -0.1875 to 0.1875
Outputs:
- evolved: float32 [36, 32, 192, 256], P('dir', 'freq', ('groups', 'space')), parts along dimension 2
There are 2 independent parts, one for each index of `groups`. A program takes and returns all parts, laid end to end along the dimension named above; an argument that names none is the same for every part. Nothing has to cross between parts.
All inputs are finite; a program needn't handle non-finite values. No bound on the sum of `land_mask` on one device may be relied on, other than what follows from the above.
Results may differ from a plain program's by a relative error of at most 0.000071.
Values sent between devices are 32-bit elements; how exact they have to be, the bound alone decides.
A program may use at most 128 MiB of HBM per device.

v0:
```python
import math

import jax
import jax.numpy as jnp
from jax import lax
from jax.sharding import PartitionSpec as P

REACH = 3


whitecap_coef = 0.01
nonlinear_coef = 0.5
small_eps = 1e-05


def extended_2(block, sides, width, periodic):
    for axis, dim in sides:
        count = lax.axis_size(axis)
        forward = [(i, i + 1) for i in range(count - 1)]
        if periodic:
            forward.append((count - 1, 0))
        backward = [(target, source) for source, target in forward]
        low = lax.ppermute(
            lax.slice_in_dim(block, block.shape[dim] - width, None, axis=dim), axis, forward
        )
        high = lax.ppermute(lax.slice_in_dim(block, 0, width, axis=dim), axis, backward)
        block = jnp.concatenate([low, block, high], axis=dim)
    return block


def frequencies(band_count):
    return 0.5 * jnp.power(1.07, jnp.arange(band_count, dtype=jnp.int32).astype(jnp.float32))


def propagate(masked, above_row, below_row, speed_x, speed_y):
    left_col = jnp.pad(masked, ((0, 0), (0, 0), (0, 0), (1, 0)))[:, :, :, :-1]
    right_col = jnp.pad(masked, ((0, 0), (0, 0), (0, 0), (0, 1)))[:, :, :, 1:]
    result = masked - jnp.maximum(speed_x, 0.0) * (masked - above_row)
    result = result - jnp.minimum(speed_x, 0.0) * (below_row - masked)
    result = result - jnp.maximum(speed_y, 0.0) * (masked - left_col)
    result = result - jnp.minimum(speed_y, 0.0) * (right_col - masked)
    return result


def turn_spectrum(padded, shifts, weights):
    dir_count = padded.shape[0] - 2 * REACH
    turned = jnp.zeros((dir_count,) + padded.shape[1:], padded.dtype)
    for offset in range(-REACH, REACH + 1):
        weight_off = jnp.where(shifts[None] == -offset, 1.0 - weights, 0.0) + jnp.where(
            shifts[None] == -offset - 1, weights, 0.0
        )
        turned = turned + weight_off[None] * padded[REACH + offset : REACH + offset + dir_count]
    return turned


def friction_lookup(depth_class, friction_table):
    onehot = (
        depth_class[None] == jnp.arange(friction_table.shape[0], dtype=jnp.int32)[:, None, None]
    ).astype(jnp.float32)
    return jnp.einsum("cf,crn->frn", friction_table, onehot, precision=lax.Precision.HIGHEST)


def sources(spectrum, sigmas, angles, wind_rate, wind_angle, friction, transfer, sea_mask):
    bin_count = spectrum.shape[0] * spectrum.shape[1]
    sigma_wide = sigmas[None, :, None, None]
    energy = jnp.sum(spectrum, axis=(0, 1)) / bin_count
    first_moment = jnp.sum(spectrum * sigma_wide, axis=(0, 1)) / bin_count
    mean_sigma = first_moment / (energy + small_eps)
    steepness = energy * mean_sigma * mean_sigma
    alignment = jnp.maximum(jnp.cos(angles[:, None, None, None] - wind_angle[None, None]), 0.0)
    wind_input = wind_rate[None, None] * alignment * sigma_wide * spectrum
    whitecap = -whitecap_coef * (steepness * steepness)[None, None] * sigma_wide * spectrum
    bottom = -friction[None] * spectrum
    flattened = spectrum.reshape(bin_count, -1)
    mixed = lax.dot_general(
        transfer,
        flattened,
        (((0,), (0,)), ((), ())),
        precision=lax.Precision.HIGHEST,
        preferred_element_type=jnp.float32,
    ).reshape(spectrum.shape)
    nonlinear = nonlinear_coef * (energy * energy)[None, None] * mixed
    return sea_mask[None, None] * (spectrum + wind_input + whitecap + bottom + nonlinear)


def shards(
    spectrum,
    land_mask,
    depth_class,
    shift_count,
    turning,
    wind_rate,
    wind_angle,
    cfl,
    freq_turn,
    friction_table,
    transfer,
):
    dir_local, freq_local, row_count, col_count = spectrum.shape
    dir_groups = lax.axis_size("dir")
    freq_groups = lax.axis_size("freq")
    dir_total = dir_local * dir_groups
    freq_total = freq_local * freq_groups
    dir_first = lax.axis_index("dir") * dir_local
    freq_first = lax.axis_index("freq") * freq_local
    sea_mask = (land_mask == 1).astype(jnp.float32)
    masked = spectrum * sea_mask[None, None]
    local_angles = (
        2.0
        * math.pi
        * (dir_first + jnp.arange(dir_local, dtype=jnp.int32)).astype(jnp.float32)
        / dir_total
    )
    local_cfl = lax.dynamic_slice_in_dim(cfl, freq_first, freq_local)
    speed_x = local_cfl[None, :, None, None] * jnp.cos(local_angles)[:, None, None, None]
    speed_y = local_cfl[None, :, None, None] * jnp.sin(local_angles)[:, None, None, None]
    extended = extended_2(masked, (("space", 2),), 1, False)
    moved = (
        propagate(masked, extended[:, :, :-2], extended[:, :, 2:], speed_x, speed_y)
        * sea_mask[None, None]
    )
    shifts_all = jnp.repeat(shift_count, col_count // shift_count.shape[1], axis=1)
    block_rows = row_count // (dir_groups * freq_groups)
    row_start = (lax.axis_index("dir") * freq_groups + lax.axis_index("freq")) * block_rows

    def rows_of(table):
        return lax.dynamic_slice_in_dim(table, row_start, block_rows, 0)

    padded = extended_2(moved, (("dir", 0),), REACH, True)
    local_turn = lax.dynamic_slice_in_dim(freq_turn, freq_first, freq_local)
    ready = turn_spectrum(padded, shifts_all, turning[None] * local_turn[:, None, None])
    gathered = lax.all_to_all(
        lax.all_to_all(ready, "dir", split_axis=2, concat_axis=0, tiled=True),
        "freq",
        split_axis=2,
        concat_axis=1,
        tiled=True,
    )
    all_angles = (
        2.0 * math.pi * jnp.arange(dir_total, dtype=jnp.int32).astype(jnp.float32) / dir_total
    )
    sigmas = frequencies(freq_total)
    friction = friction_lookup(rows_of(depth_class), friction_table)
    updated = sources(
        gathered,
        sigmas,
        all_angles,
        rows_of(wind_rate),
        rows_of(wind_angle),
        friction,
        transfer,
        rows_of(sea_mask),
    )
    evolved = lax.all_to_all(
        lax.all_to_all(updated, "freq", split_axis=1, concat_axis=2, tiled=True),
        "dir",
        split_axis=0,
        concat_axis=2,
        tiled=True,
    )
    return evolved


def solution(mesh):
    in_specs = (
        P("dir", "freq", ("groups", "space"), None),
        P(("groups", "space"), None),
        P(("groups", "space"), None),
        P(("groups", "space"), None),
        P(("groups", "space"), None),
        P(("groups", "space"), None),
        P(("groups", "space"), None),
        P(),
        P(),
        P(),
        P(),
    )
    out_specs = P("dir", "freq", ("groups", "space"), None)
    return jax.shard_map(shards, mesh=mesh, in_specs=in_specs, out_specs=out_specs, check_vma=False)
```

profile of v0, /device:TPU:0, one launch (start us, length us, event | category | flops | bytes accessed | tf_op | source)
XLA Modules:
  0.0 431.0 jit_solution(13730932830140669563)
XLA Ops:
  0.8 5.3 %copy_multiply_fusion.1 = f32[18,16,24,256]{3,1,0,2:T(8,128)S(1)} fusion(f32[18,16,24,256]{3,2,1,0:T(8,128)} %param.11, f32[24,256]{1,0:T(8,128)S(1)} %compare_convert_fusion), kind=kLoop, calls=%fused_computation.52 | loop fusion | flops 1769472 | bytes 14180352 | tf_op jit(solution)/shard_map/mul | solution.py:107
  6.1 3.0 copy-done.5
  9.1 4.9 %collective-permute-start = (f32[18,16,1,256]{3,1,0,2:T(8,128)S(1)}, f32[18,16,1,256]{3,1,0,2:T(8,128)S(1)}, u32[]{:S(2)}, u32[]{:S(2)}) collective-permute-start(f32[18,16,1,256]{3,1,0,2:T(8,128)S(1)} %get-tuple-element.9), channel_id=1, source_target_pairs={{0,2},{2,4},{4,6},{1,3},{3,5},{5,7},{8,10},{10,12},{12,14},{9,11},... | collective-permute-start | bytes 884744 | tf_op jit(solution)/shard_map/ppermute | solution.py:23
  14.0 1.3 collective-permute-start.1
  15.5 4.7 %collective-permute-done = f32[18,16,1,256]{3,1,0,2:T(8,128)S(1)} collective-permute-done((f32[18,16,1,256]{3,1,0,2:T(8,128)S(1)}, f32[18,16,1,256]{3,1,0,2:T(8,128)S(1)}, u32[]{:S(2)}, u32[]{:S(2)}) %collective-permute-start) | collective-permute-done | bytes 294944 | tf_op jit(solution)/shard_map/ppermute | solution.py:23
  20.2 4.1 collective-permute-done.1
  24.4 13.4 %fusion.18 = f32[18,16,24,256]{3,1,0,2:T(8,128)S(1)} fusion(f32[18,16,24,256]{3,1,0,2:T(8,128)} %copy-done.5, f32[18,16,1,256]{3,1,0,2:T(8,128)S(1)} %collective-permute-done.1, f32[18,16,1,256]{3,1,0,2:T(8,128)S(1)} %collective-permute-done, f32[18,16]{1,0:T(8,128)S(1)} %get-tuple-element.32, f32[18,16]{1,0:T(8,128)S(1)} %get-tuple-element.33, ...), kind=kLoop, calls=%fused_computation.30 | loop fusion | flops 26542080 | bytes 14774784 | tf_op jit(solution)/shard_map/mul | solution.py:119
  37.8 3.0 copy-done.3
  40.8 1.7 fusion.54
  42.5 1.5 collective-permute-start.2
  47.6 24.1 %collective-permute-done.2 = f32[3,16,24,256]{3,1,0,2:T(8,128)} collective-permute-done((f32[3,16,24,256]{3,1,0,2:T(8,128)}, f32[3,16,24,256]{3,1,0,2:T(8,128)}, u32[]{:S(2)}, u32[]{:S(2)}) %collective-permute-start.2) | collective-permute-done | bytes 1179680 | tf_op jit(solution)/shard_map/ppermute | solution.py:23
  71.7 22.9 %collective-permute-done.3 = f32[3,16,24,256]{3,1,0,2:T(8,128)} collective-permute-done((f32[3,16,24,256]{3,1,0,2:T(8,128)}, f32[3,16,24,256]{3,1,0,2:T(8,128)}, u32[]{:S(2)}, u32[]{:S(2)}) %collective-permute-start.3) | collective-permute-done | bytes 1179680 | tf_op jit(solution)/shard_map/ppermute | solution.py:26
  94.6 20.9 %fusion.3 = f32[18,16,24,256]{3,1,0,2:T(8,128)} fusion(f32[18,16,24,256]{3,1,0,2:T(8,128)} %copy-done.3, f32[3,16,24,256]{3,1,0,2:T(8,128)} %collective-permute-done.3, f32[3,16,24,256]{3,1,0,2:T(8,128)} %collective-permute-done.2, f32[16,24,256]{2,0,1:T(8,128)S(1)} %get-tuple-element.17, f32[16,24,256]{2,0,1:T(8,128)S(1)} %get-tuple-element.16, ...), kind=kLoop, calls=%fused_computation.15 | loop fusion | flops 33619968 | bytes 19267584 | tf_op jit(solution)/shard_map/add | solution.py:52
  115.5 7.1 %all-to-all-start = ((f32[18,16,24,256]{3,1,0,2:T(8,128)}), f32[18,16,24,256]{3,1,0,2:T(8,128)}, u32[]{:S(2)}, u32[]{:S(2)}) async-start(f32[18,16,24,256]{3,1,0,2:T(8,128)} %fusion.3), calls=%async_computation | async-start | bytes 14155776 | tf_op jit(solution)/shard_map/all_to_all | solution.py:133
  124.8 74.3 %all-to-all-done = f32[18,16,24,256]{3,1,0,2:T(8,128)} async-done(((f32[18,16,24,256]{3,1,0,2:T(8,128)}), f32[18,16,24,256]{3,1,0,2:T(8,128)}, u32[]{:S(2)}, u32[]{:S(2)}) %all-to-all-start) | async-done | bytes 7077920 | tf_op jit(solution)/shard_map/all_to_all | solution.py:133
  199.1 3.8 copy.70
  203.7 9.4 %all_to_all.72 = f32[36,16,12,256]{3,1,0,2:T(8,128)S(1)} all-to-all(f32[36,16,12,256]{3,1,0,2:T(8,128)S(1)} %copy.71), channel_id=1, replica_groups=mesh['groups'=2,'dir'=2,'space'=4,'freq'=2] {'freq'}, dimensions={2} | all-to-all | bytes 14155776 | tf_op jit(solution)/shard_map/all_to_all | solution.py:132
  213.2 4.2 copy.73
  218.1 6.8 %copy.74 = f32[36,2,16,6,256]{4,3,2,1,0:T(8,128)S(1)} copy(f32[36,2,16,6,256]{4,2,0,3,1:T(8,128)S(1)} %bitcast.38) | data formatting | bytes 14155776 | tf_op jit(solution)/shard_map/all_to_all | solution.py:132
  224.9 3.5 copy.86
  228.4 61.7 %convolution_bitcast_fusion = f32[1152,1536]{0,1:T(8,128)} fusion(f32[1152,1536]{1,0:T(8,128)S(1)} %bitcast.46, f32[1152,1152]{1,0:T(8,128)} %param.21), kind=kOutput, calls=%fused_computation.7 | convolution fusion | flops 24461180928 | bytes 19464192 | tf_op jit(solution)/shard_map/dot_general | solution.py:75
  290.1 8.0 %copy.75 = f32[1152,1536]{1,0:T(8,128)} copy(f32[1152,1536]{0,1:T(8,128)} %convolution_bitcast_fusion) | data formatting | bytes 14155776 | tf_op jit(solution)/shard_map/dot_general | solution.py:75
  298.2 9.6 %reshape.279 = f32[36,32,6,256]{3,2,1,0:T(8,128)} reshape(f32[1152,1536]{1,0:T(8,128)} %copy.75) | data formatting | bytes 14155776 | tf_op jit(solution)/shard_map/reshape | solution.py:81
  307.8 4.0 copy.72
  311.8 1.3 multiply_reduce_fusion
  313.4 6.8 %fusion.24 = f32[36,32,6,256]{3,1,2,0:T(8,128)S(1)} fusion(f32[36,2,16,6,256]{4,2,1,3,0:T(8,128)} %copy.73, f32[36,32,6,256]{3,2,1,0:T(8,128)S(1)} %copy-done.4, f32[6,256]{1,0:T(8,128)S(1)} %get-tuple-element.19, f32[32,6,256]{2,0,1:T(8,128)S(1)} %fusion.40, f32[32,6,256]{2,0,1:T(8,128)S(1)} %broadcast_multiply_fusion, f32[32]{0:T(128)S(1)} %power_multiply_fusion.1, ...), kind=kLoop, calls=%fused_computation.36 | loop fusion | flops 17694720 | bytes 21860480 | tf_op jit(solution)/shard_map/mul | solution.py:83
  320.3 4.1 copy.77
  324.4 10.3 %all_to_all.73 = f32[36,32,6,256]{3,0,2,1:T(8,128)S(1)} all-to-all(f32[36,32,6,256]{3,0,2,1:T(8,128)S(1)} %copy.77), channel_id=1, replica_groups=mesh['groups'=2,'dir'=2,'space'=4,'freq'=2] {'freq'}, dimensions={1} | all-to-all | bytes 14155776 | tf_op jit(solution)/shard_map/all_to_all | solution.py:155
  334.7 4.1 copy.79
  338.8 81.8 %all_to_all.74 = f32[36,16,12,256]{3,1,2,0:T(8,128)S(1)} all-to-all(f32[36,16,12,256]{3,1,2,0:T(8,128)S(1)} %bitcast.41), channel_id=1, replica_groups=mesh['groups'=2,'dir'=2,'space'=4,'freq'=2] {'dir'}, dimensions={0} | all-to-all | bytes 14155776 | tf_op jit(solution)/shard_map/all_to_all | solution.py:154
  420.6 1.3 copy.80
  422.0 8.6 %copy.81 = f32[18,16,24,256]{3,2,1,0:T(8,128)} copy(f32[18,16,24,256]{3,1,2,0:T(8,128)S(1)} %bitcast.44) | data formatting | bytes 14155776 | tf_op jit(solution)/shard_map/all_to_all | solution.py:154
  (64 shorter events, 8.6 us)
Async XLA Ops:
  0.0 122.7 %copy-start = (s32[24,256]{1,0:T(8,128)S(1)}, s32[24,256]{1,0:T(8,128)}, u32[]{:S(2)}) copy-start(s32[24,256]{1,0:T(8,128)} %param.13) | copy-start | bytes 73732
  0.8 14.6 %copy-start.9 = (f32[32]{0:T(128)S(1)}, f32[32]{0:T(128)}, u32[]{:S(2)}) copy-start(f32[32]{0:T(128)} %param.18) | copy-start | bytes 388
  6.0 3.0 copy-start.5
  9.1 11.2 %collective-permute-start = (f32[18,16,1,256]{3,1,0,2:T(8,128)S(1)}, f32[18,16,1,256]{3,1,0,2:T(8,128)S(1)}, u32[]{:S(2)}, u32[]{:S(2)}) collective-permute-start(f32[18,16,1,256]{3,1,0,2:T(8,128)S(1)} %get-tuple-element.9), channel_id=1, source_target_pairs={{0,2},{2,4},{4,6},{1,3},{3,5},{5,7},{8,10},{10,12},{12,14},{9,11},... | collective-permute-start | bytes 884744 | tf_op jit(solution)/shard_map/ppermute | solution.py:23
  14.0 10.4 %collective-permute-start.1 = (f32[18,16,1,256]{3,1,0,2:T(8,128)S(1)}, f32[18,16,1,256]{3,1,0,2:T(8,128)S(1)}, u32[]{:S(2)}, u32[]{:S(2)}) collective-permute-start(f32[18,16,1,256]{3,1,0,2:T(8,128)S(1)} %get-tuple-element.10), channel_id=1, source_target_pairs={{2,0},{4,2},{6,4},{3,1},{5,3},{7,5},{10,8},{12,10},{14,12},{11,9},... | collective-permute-start | bytes 884744 | tf_op jit(solution)/shard_map/ppermute | solution.py:26
  24.4 20.1 %copy-start.10 = (f32[32]{0:T(128)S(1)}, f32[32]{0:T(128)}, u32[]{:S(2)}) copy-start(f32[32]{0:T(128)} %param.19) | copy-start | bytes 388
  24.4 20.2 %copy-start.7 = (s32[24,8]{0,1:T(8,128)S(1)}, s32[24,8]{0,1:T(8,128)}, u32[]{:S(2)}) copy-start(s32[24,8]{0,1:T(8,128)} %param.14) | copy-start | bytes 2308
  24.4 22.6 %copy-start.6 = (f32[24,256]{1,0:T(8,128)S(1)}, f32[24,256]{1,0:T(8,128)}, u32[]{:S(2)}) copy-start(f32[24,256]{1,0:T(8,128)} %param.15) | copy-start | bytes 73732
  37.8 3.0 copy-start.3
  42.5 29.2 %collective-permute-start.2 = (f32[3,16,24,256]{3,1,0,2:T(8,128)}, f32[3,16,24,256]{3,1,0,2:T(8,128)}, u32[]{:S(2)}, u32[]{:S(2)}) collective-permute-start(f32[3,16,24,256]{3,1,0,2:T(8,128)} %get-tuple-element.7), channel_id=1, source_target_pairs={{0,8},{8,0},{1,9},{9,1},{2,10},{10,2},{3,11},{11,3},{4,12},{12,4},... | collective-permute-start | bytes 3538952 | tf_op jit(solution)/shard_map/ppermute | solution.py:23
  44.0 50.6 %collective-permute-start.3 = (f32[3,16,24,256]{3,1,0,2:T(8,128)}, f32[3,16,24,256]{3,1,0,2:T(8,128)}, u32[]{:S(2)}, u32[]{:S(2)}) collective-permute-start(f32[3,16,24,256]{3,1,0,2:T(8,128)} %get-tuple-element.8), channel_id=1, source_target_pairs={{8,0},{0,8},{9,1},{1,9},{10,2},{2,10},{11,3},{3,11},{12,4},{4,12},... | collective-permute-start | bytes 3538952 | tf_op jit(solution)/shard_map/ppermute | solution.py:26
  115.5 8.0 %copy-start.8 = (f32[8,32]{1,0:T(8,128)S(1)}, f32[8,32]{1,0:T(8,128)}, u32[]{:S(2)}) copy-start(f32[8,32]{1,0:T(8,128)} %param.20) | copy-start | bytes 3076
  115.5 83.5 %all-to-all-start = ((f32[18,16,24,256]{3,1,0,2:T(8,128)}), f32[18,16,24,256]{3,1,0,2:T(8,128)}, u32[]{:S(2)}, u32[]{:S(2)}) async-start(f32[18,16,24,256]{3,1,0,2:T(8,128)} %fusion.3), calls=%async_computation | async-start | bytes 14155776 | tf_op jit(solution)/shard_map/all_to_all | solution.py:133
  213.2 5.0 %copy-start.2 = (f32[36,16,12,256]{3,1,0,2:T(8,128)}, f32[36,16,12,256]{3,1,0,2:T(8,128)S(1)}, u32[]{:S(2)}) copy-start(f32[36,16,12,256]{3,1,0,2:T(8,128)S(1)} %all_to_all.72) | copy-start | bytes 21233668
  307.8 5.7 %copy-start.4 = (f32[36,32,6,256]{3,2,1,0:T(8,128)S(1)}, f32[36,32,6,256]{3,2,1,0:T(8,128)}, u32[]{:S(2)}) copy-start(f32[36,32,6,256]{3,2,1,0:T(8,128)} %reshape.279) | copy-start | bytes 21233668
  421.9 8.7 %copy-start.1 = (s32[24,256]{1,0:T(8,128)S(1)}, s32[24,256]{1,0:T(8,128)}, u32[]{:S(2)}) copy-start(s32[24,256]{1,0:T(8,128)} %param.13) | copy-start | bytes 73732
where the time goes:
time: 438 us; the launch traced here: 431 us
  waiting for transfers between devices  130 us (30%)
  blocking collectives  101 us (23%)
  local copies, waits for them, and re-layouts  71 us (16%)
  matrix products  62 us (14%)
  other arithmetic  50.4 us (12%)
  starting transfers between devices  15.4 us (4%)
    all_to_all x1, blocking collectives, shards(): lax.all_to_all(lax.all_to_all(updated, 'freq', split_axis=1, concat_axis=...  81.8 us
    all_to_all x1, waiting for transfers between devices, shards(): lax.all_to_all(ready, 'dir', split_axis=2, concat_axis=0, tiled=True)  74.3 us
    dot_general x1, matrix products, sources(): lax.dot_general(transfer, flattened, (((0,), (0,)), ((), ())), precision=...  61.7 us
    ppermute x2, waiting for transfers between devices, extended_2(): lax.ppermute(lax.slice_in_dim(block, block.shape[dim] - width, None, axis...  28.8 us
    ppermute x2, waiting for transfers between devices, extended_2(): lax.ppermute(lax.slice_in_dim(block, 0, width, axis=dim), axis, backward)  27 us
    add x1, other arithmetic, turn_spectrum(): turned + weight_off[None] * padded[REACH + offset:REACH + offset + dir_co...  20.9 us
    all_to_all x3, local copies, waits for them, and re-layouts, shards(): lax.all_to_all(lax.all_to_all(ready, 'dir', split_axis=2, concat_axis=0,...  15.1 us
    mul x1, other arithmetic, shards(): propagate(masked, extended[:, :, :-2], extended[:, :, 2:], speed_x, speed_y)  13.4 us
  transfers between devices with their start and end apart: 5, of which 5 were waited for; matrix products, arithmetic and copies ran while one was open for 1% of the time, Pallas kernels for 0%

commit v1 on v0

v1 whole, which is shorter than its diff:
```python
import functools
import math

import jax
import jax.numpy as jnp
import numpy as np
from jax import lax
from jax.experimental import pallas as pl
from jax.experimental.pallas import tpu as pltpu
from jax.sharding import PartitionSpec as P

ROWS = 8
LANES = 128
MESH_ID = pl.DeviceIdType.MESH

whitecap_coef = 0.01
nonlinear_coef = 0.5
small_eps = 1e-05


def kernel(
    dir_groups,
    space_groups,
    spec_ref,
    land_ref,
    depth_ref,
    shift_ref,
    turning_ref,
    rate_ref,
    wind_ref,
    cfl_ref,
    turn_ref,
    fric_ref,
    cos_ref,
    sin_ref,
    sigma_ref,
    transfer_ref,
    out_ref,
    grid_buf,
    turned_buf,
    own_part,
    send_part,
    recv_part,
    out_buf,
    matrix,
    raw_matrix,
    edge_top,
    edge_bot,
    halo_up,
    halo_dn,
    sea_ref,
    shift_wide,
    coswind,
    sinwind,
    matrix_sem,
    halo_send,
    halo_recv,
    dir_send,
    dir_recv,
    part_send,
    part_recv,
    out_sem,
):
    me_dir = lax.axis_index("dir")
    me_space = lax.axis_index("space")
    me_freq = lax.axis_index("freq")
    other_freq = 1 - me_freq
    dir_total, freq_local = grid_buf.shape[1], grid_buf.shape[2]
    dir_local = dir_total // dir_groups
    bins = dir_local * freq_local
    row_count = out_ref.shape[1]
    col_count = out_ref.shape[2]
    tiles = row_count // ROWS
    halves = col_count // LANES
    chunks = tiles * halves
    class_count = fric_ref.shape[0]
    bin_total = transfer_ref.shape[2]
    dir_first = me_dir * dir_local
    freq_first = pl.multiple_of(me_freq * freq_local, 8)

    barrier = pltpu.get_barrier_semaphore()
    for j in range(1, dir_groups):
        pl.semaphore_signal(
            barrier, inc=1, device_id={"dir": lax.rem(me_dir + j, dir_groups)}, device_id_type=MESH_ID
        )
    pl.semaphore_signal(barrier, inc=1, device_id={"freq": other_freq}, device_id_type=MESH_ID)

    @pl.when(me_space > 0)
    def _():
        pl.semaphore_signal(barrier, inc=1, device_id={"space": me_space - 1}, device_id_type=MESH_ID)

    @pl.when(me_space < space_groups - 1)
    def _():
        pl.semaphore_signal(barrier, inc=1, device_id={"space": me_space + 1}, device_id_type=MESH_ID)

    matrix_copy = pltpu.make_async_copy(
        transfer_ref.at[:, pl.ds(freq_first, freq_local), :], raw_matrix, matrix_sem
    )
    matrix_copy.start()

    sea_ref[...] = jnp.where(land_ref[...] == 1, 1.0, 0.0)

    first_sea = sea_ref[pl.ds(0, ROWS), :]
    last_sea = sea_ref[pl.ds(row_count - ROWS, ROWS), :]

    def pack(b, carry):
        base = pl.multiple_of(b * row_count, ROWS)
        top = spec_ref[pl.ds(base, ROWS), :] * first_sea
        low = spec_ref[pl.ds(base + row_count - ROWS, ROWS), :] * last_sea
        edge_top[pl.ds(b, 1), :] = top[:1]
        edge_bot[pl.ds(b, 1), :] = low[ROWS - 1 :]
        return carry

    lax.fori_loop(0, bins, pack, 0, unroll=8)

    pl.semaphore_wait(
        barrier,
        dir_groups
        + (me_space > 0).astype(jnp.int32)
        + (me_space < space_groups - 1).astype(jnp.int32),
    )

    up_copy = pltpu.make_async_remote_copy(
        src_ref=edge_top,
        dst_ref=halo_dn,
        send_sem=halo_send.at[0],
        recv_sem=halo_recv.at[0],
        device_id={"space": jnp.maximum(me_space - 1, 0)},
        device_id_type=MESH_ID,
    )
    down_copy = pltpu.make_async_remote_copy(
        src_ref=edge_bot,
        dst_ref=halo_up,
        send_sem=halo_send.at[1],
        recv_sem=halo_recv.at[1],
        device_id={"space": jnp.minimum(me_space + 1, space_groups - 1)},
        device_id_type=MESH_ID,
    )

    @pl.when(me_space > 0)
    def _():
        up_copy.start()

    @pl.when(me_space < space_groups - 1)
    def _():
        down_copy.start()

    def dir_copy(c, j):
        region = grid_buf.at[c, pl.ds(dir_first, dir_local)]
        return pltpu.make_async_remote_copy(
            src_ref=region,
            dst_ref=region,
            send_sem=dir_send.at[c, j - 1],
            recv_sem=dir_recv.at[c, j - 1],
            device_id={"dir": lax.rem(me_dir + j, dir_groups)},
            device_id_type=MESH_ID,
        )

    row_id = lax.broadcasted_iota(jnp.int32, (ROWS, col_count), 0)
    col_id = lax.broadcasted_iota(jnp.int32, (ROWS, col_count), 1)

    def propagate(tile, place):
        sea = sea_ref[pl.ds(tile * ROWS, ROWS), :]
        if tile > 0:
            sea_prev = sea_ref[pl.ds(tile * ROWS - ROWS, ROWS), :]
        if tile < tiles - 1:
            sea_next = sea_ref[pl.ds(tile * ROWS + ROWS, ROWS), :]

        def per_dir(d, carry):
            cos_d = cos_ref[dir_first + d]
            sin_d = sin_ref[dir_first + d]

            def per_freq(f, inner):
                b = d * freq_local + f
                base = pl.multiple_of(b * row_count, ROWS)
                here = spec_ref[pl.ds(base + tile * ROWS, ROWS), :] * sea
                if tile > 0:
                    prev = spec_ref[pl.ds(base + (tile - 1) * ROWS, ROWS), :] * sea_prev
                    above = pltpu.roll(jnp.where(row_id == ROWS - 1, prev, here), 1, 0)
                else:
                    above = jnp.where(row_id == 0, halo_up[pl.ds(b, 1), :], pltpu.roll(here, 1, 0))
                if tile < tiles - 1:
                    later = spec_ref[pl.ds(base + (tile + 1) * ROWS, ROWS), :] * sea_next
                    below = pltpu.roll(jnp.where(row_id == 0, later, here), ROWS - 1, 0)
                else:
                    below = jnp.where(
                        row_id == ROWS - 1, halo_dn[pl.ds(b, 1), :], pltpu.roll(here, ROWS - 1, 0)
                    )
                left = jnp.where(col_id == 0, 0.0, pltpu.roll(here, 1, 1))
                right = jnp.where(col_id == col_count - 1, 0.0, pltpu.roll(here, col_count - 1, 1))
                speed = cfl_ref[freq_first + f]
                speed_x = speed * cos_d
                speed_y = speed * sin_d
                moved = here - jnp.maximum(speed_x, 0.0) * (here - above)
                moved = moved - jnp.minimum(speed_x, 0.0) * (below - here)
                moved = moved - jnp.maximum(speed_y, 0.0) * (here - left)
                moved = moved - jnp.minimum(speed_y, 0.0) * (right - here)
                moved = moved * sea
                for h in range(halves):
                    grid_buf[place * halves + h, dir_first + d, f] = moved[:, h * LANES : (h + 1) * LANES]
                return inner

            return lax.fori_loop(0, freq_local, per_freq, carry, unroll=4)

        lax.fori_loop(0, dir_local, per_dir, 0)
        for h in range(halves):
            for j in range(1, dir_groups):
                dir_copy(place * halves + h, j).start()

    for place in range(tiles - 2):
        propagate(place + 1, place)

    @pl.when(me_space > 0)
    def _():
        up_copy.wait_send()
        down_copy.wait_recv()

    @pl.when(me_space == 0)
    def _():
        halo_up[...] = jnp.zeros_like(halo_up)

    @pl.when(me_space < space_groups - 1)
    def _():
        down_copy.wait_send()
        up_copy.wait_recv()

    @pl.when(me_space == space_groups - 1)
    def _():
        halo_dn[...] = jnp.zeros_like(halo_dn)

    propagate(0, tiles - 2)
    propagate(tiles - 1, tiles - 1)

    coswind[...] = jnp.cos(wind_ref[...])
    sinwind[...] = jnp.sin(wind_ref[...])
    table_cols = lax.broadcasted_iota(jnp.int32, (row_count, col_count), 1)
    shift_tiles = shift_ref.shape[1]
    width = col_count // shift_tiles
    wide = jnp.zeros((row_count, col_count), jnp.int32)
    for s in range(shift_tiles):
        inside = (table_cols >= s * width) & (table_cols < (s + 1) * width)
        wide = jnp.where(inside, jnp.broadcast_to(shift_ref[:, s : s + 1], wide.shape), wide)
    shift_wide[...] = wide

    matrix_copy.wait()
    depth = dir_total * freq_local
    for m in range(bin_total // LANES):
        block = raw_matrix[:, :, m * LANES : (m + 1) * LANES].reshape(depth, LANES)
        high = block.astype(jnp.bfloat16).astype(jnp.float32)
        low = block - high
        turned_block = jnp.concatenate([high, low, high], axis=0).T.astype(jnp.bfloat16)
        for piece in range(LANES // freq_local):
            d, g = divmod(m * (LANES // freq_local) + piece, 2)
            matrix[g, pl.ds(d * freq_local, freq_local), :] = turned_block[
                piece * freq_local : (piece + 1) * freq_local
            ]

    def chunk(c, carry):
        place = c // halves
        half = c % halves
        tile = jnp.where(place < tiles - 2, place + 1, jnp.where(place == tiles - 2, 0, tiles - 1))
        rows = pl.ds(pl.multiple_of(tile * ROWS, ROWS), ROWS)
        cols = pl.ds(pl.multiple_of(half * LANES, LANES), LANES)
        for j in range(1, dir_groups):
            dir_copy(c, j).wait_recv()

        shift = shift_wide[rows, cols]
        turning = turning_ref[rows, cols]
        picks = [shift == k for k in range(-2, 2)]

        def refract(f, sums):
            weight = turning * turn_ref[freq_first + f]
            rest = 1.0 - weight
            moved = [grid_buf[c, d, f] for d in range(dir_total)]

            def shifted(d):
                result = moved[(d - 2) % dir_total]
                for k in (1, 0, -1, -2):
                    result = jnp.where(picks[k + 2], moved[(d - k) % dir_total], result)
                return result

            before = shifted(-1)
            total = jnp.zeros((ROWS, LANES), jnp.float32)
            for d in range(dir_total):
                now = shifted(d)
                turned = rest * now + weight * before
                turned_buf[pl.ds(pl.multiple_of((d * freq_local + f) * ROWS, ROWS), ROWS), :] = turned
                total = total + turned
                before = now
            return sums[0] + total, sums[1] + total * sigma_ref[freq_first + f]

        zero = jnp.zeros((ROWS, LANES), jnp.float32)
        energy, moment = lax.fori_loop(0, freq_local, refract, (zero, zero))
        send_part[pl.ds(bins * ROWS, ROWS), :] = energy
        send_part[pl.ds((bins + 1) * ROWS, ROWS), :] = moment

        mine = pl.ds(pl.multiple_of(dir_first * freq_local, 16), bins)

        def mix(pair, inner):
            first = turned_buf[pl.ds(2 * pair, depth, stride=ROWS), :]
            second = turned_buf[pl.ds(2 * pair + 1, depth, stride=ROWS), :]
            both = jnp.concatenate([first, second], axis=1)
            high = both.astype(jnp.bfloat16)
            low = (both - high.astype(jnp.float32)).astype(jnp.bfloat16)
            right = jnp.concatenate([high, high, low], axis=0)
            left = jnp.concatenate([matrix[me_freq, mine, :], matrix[other_freq, mine, :]], axis=0)
            part = jnp.dot(left, right, preferred_element_type=jnp.float32)
            own_part[pl.ds(2 * pair, bins, stride=ROWS), :] = part[:bins, :LANES]
            own_part[pl.ds(2 * pair + 1, bins, stride=ROWS), :] = part[:bins, LANES:]
            send_part[pl.ds(2 * pair, bins, stride=ROWS), :] = part[bins:, :LANES]
            send_part[pl.ds(2 * pair + 1, bins, stride=ROWS), :] = part[bins:, LANES:]
            return inner

        lax.fori_loop(0, ROWS // 2, mix, 0)
        swap = pltpu.make_async_remote_copy(
            src_ref=send_part,
            dst_ref=recv_part.at[c],
            send_sem=part_send.at[c],
            recv_sem=part_recv.at[c],
            device_id={"freq": other_freq},
            device_id_type=MESH_ID,
        )
        swap.start()
        swap.wait()

        sea = sea_ref[rows, cols]
        energy = (energy + recv_part[c, pl.ds(bins * ROWS, ROWS), :]) / bin_total
        moment = (moment + recv_part[c, pl.ds((bins + 1) * ROWS, ROWS), :]) / bin_total
        mean_sigma = moment / (energy + small_eps)
        steepness = energy * mean_sigma * mean_sigma
        white = whitecap_coef * (steepness * steepness)
        nonlinear = sea * (nonlinear_coef * (energy * energy))
        rate = sea * rate_ref[rows, cols]
        cos_w = coswind[rows, cols]
        sin_w = sinwind[rows, cols]
        classes = depth_ref[rows, cols]

        def source(f, inner):
            sigma = sigma_ref[freq_first + f]
            friction = jnp.full((ROWS, LANES), fric_ref[0, freq_first + f], jnp.float32)
            for k in range(1, class_count):
                friction = jnp.where(classes == k, fric_ref[k, freq_first + f], friction)
            keep = sea * (1.0 - white * sigma - friction)
            grow = rate * sigma
            for d in range(dir_local):
                at = pl.ds(pl.multiple_of((d * freq_local + f) * ROWS, ROWS), ROWS)
                whole = pl.ds(pl.multiple_of(((dir_first + d) * freq_local + f) * ROWS, ROWS), ROWS)
                align = jnp.maximum(cos_ref[dir_first + d] * cos_w + sin_ref[dir_first + d] * sin_w, 0.0)
                mixed = own_part[at, :] + recv_part[c, at, :]
                out_buf[c, d * freq_local + f] = (
                    turned_buf[whole, :] * (keep + grow * align) + nonlinear * mixed
                )
            return inner

        lax.fori_loop(0, freq_local, source, 0)
        out_copy(c, rows, cols).start()
        return carry

    def out_copy(c, rows, cols):
        return pltpu.make_async_copy(out_buf.at[c], out_ref.at[:, rows, cols], out_sem.at[c])

    lax.fori_loop(0, chunks, chunk, 0)

    def finish(c, carry):
        for j in range(1, dir_groups):
            dir_copy(c, j).wait_send()
        out_copy(c, pl.ds(0, ROWS), pl.ds(0, LANES)).wait()
        return carry

    lax.fori_loop(0, chunks, finish, 0)


def shards(
    dir_groups,
    space_groups,
    spectrum,
    land_mask,
    depth_class,
    shift_count,
    turning,
    wind_rate,
    wind_angle,
    cfl,
    freq_turn,
    friction_table,
    transfer,
):
    dir_local, freq_local, row_count, col_count = spectrum.shape
    bins = dir_local * freq_local
    dir_total = dir_local * dir_groups
    freq_total = cfl.shape[0]
    angles = 2.0 * math.pi * np.arange(dir_total) / dir_total
    cosines = jnp.asarray(np.cos(angles), jnp.float32)
    sines = jnp.asarray(np.sin(angles), jnp.float32)
    sigmas = jnp.asarray(0.5 * np.power(1.07, np.arange(freq_total)), jnp.float32)
    chunks = (row_count // ROWS) * (col_count // LANES)
    depth = dir_total * freq_local
    peers = max(dir_groups - 1, 1)
    vmem = pl.BlockSpec(memory_space=pltpu.VMEM)
    smem = pl.BlockSpec(memory_space=pltpu.SMEM)
    anywhere = pl.BlockSpec(memory_space=pl.ANY)
    f32 = jnp.float32
    evolved = pl.pallas_call(
        functools.partial(kernel, dir_groups, space_groups),
        out_shape=jax.ShapeDtypeStruct((bins, row_count, col_count), f32),
        in_specs=[vmem] * 7 + [smem] * 6 + [anywhere],
        out_specs=anywhere,
        scratch_shapes=[
            pltpu.VMEM((chunks, dir_total, freq_local, ROWS, LANES), f32),
            pltpu.VMEM((depth * ROWS, LANES), f32),
            pltpu.VMEM((bins * ROWS, LANES), f32),
            pltpu.VMEM(((bins + 2) * ROWS, LANES), f32),
            pltpu.VMEM((chunks, (bins + 2) * ROWS, LANES), f32),
            pltpu.VMEM((chunks, bins, ROWS, LANES), f32),
            pltpu.VMEM((2, depth, 3 * depth), jnp.bfloat16),
            pltpu.VMEM((dir_total, freq_local, transfer.shape[1]), f32),
            pltpu.VMEM((bins, col_count), f32),
            pltpu.VMEM((bins, col_count), f32),
            pltpu.VMEM((bins, col_count), f32),
            pltpu.VMEM((bins, col_count), f32),
            pltpu.VMEM((row_count, col_count), f32),
            pltpu.VMEM((row_count, col_count), jnp.int32),
            pltpu.VMEM((row_count, col_count), f32),
            pltpu.VMEM((row_count, col_count), f32),
            pltpu.SemaphoreType.DMA,
            pltpu.SemaphoreType.DMA((2,)),
            pltpu.SemaphoreType.DMA((2,)),
            pltpu.SemaphoreType.DMA((chunks, peers)),
            pltpu.SemaphoreType.DMA((chunks, peers)),
            pltpu.SemaphoreType.DMA((chunks,)),
            pltpu.SemaphoreType.DMA((chunks,)),
            pltpu.SemaphoreType.DMA((chunks,)),
        ],
        compiler_params=pltpu.CompilerParams(
            collective_id=0, has_side_effects=True, vmem_limit_bytes=60 * 1024 * 1024
        ),
        name="wave_step",
    )(
        spectrum.reshape(bins * row_count, col_count),
        land_mask,
        depth_class,
        shift_count,
        turning,
        wind_rate,
        wind_angle,
        cfl,
        freq_turn,
        friction_table,
        cosines,
        sines,
        sigmas,
        transfer.reshape(dir_total, freq_total, transfer.shape[1]),
    )
    return evolved.reshape(spectrum.shape)


def solution(mesh):
    points = P(("groups", "space"), None)
    in_specs = (P("dir", "freq", ("groups", "space"), None),) + (points,) * 6 + (P(),) * 4
    return jax.shard_map(
        functools.partial(shards, mesh.shape["dir"], mesh.shape["space"]),
        mesh=mesh,
        in_specs=in_specs,
        out_specs=P("dir", "freq", ("groups", "space"), None),
        check_vma=False,
    )
```

time: 438 us -> 183 us (0.42); the launches traced: 431 us -> 183 us
  Pallas kernels: 0 us -> 175 us
  waiting for transfers between devices: 130 us -> 0 us
  blocking collectives: 101 us -> 0 us
  local copies, waits for them, and re-layouts: 71 us -> 7.96 us
  matrix products: 62 us -> 0 us
  other arithmetic: 50.4 us -> 0 us
  starting transfers between devices: 15.4 us -> 0 us
    pallas_call x0 -> x1, Pallas kernels: none -> 175 us  [shards(): pl.pallas_call(functools.partial(kernel, dir_groups, space_groups), out_s...]
    all_to_all x3 -> x0, blocking collectives: 101 us -> none  [the longest x1 81.8 us: shards(): lax.all_to_all(lax.all_to_all(updated, 'freq', split_axis=1, concat_axis=...]
    all_to_all x1 -> x0, waiting for transfers between devices: 74.3 us -> none  [shards(): lax.all_to_all(ready, 'dir', split_axis=2, concat_axis=0, tiled=True)]
    dot_general x2 -> x0, matrix products: 62 us -> none  [the longest x1 61.7 us: sources(): lax.dot_general(transfer, flattened, (((0,), (0,)), ((), ())), precision=...]
    ppermute x4 -> x0, waiting for transfers between devices: 55.8 us -> none  [the longest x2 28.8 us: extended_2(): lax.ppermute(lax.slice_in_dim(block, block.shape[dim] - width, None, axis...]
    all_to_all x8 -> x0, local copies, waits for them, and re-layouts: 33.8 us -> none  [the longest x3 15.1 us: shards(): lax.all_to_all(lax.all_to_all(ready, 'dir', split_axis=2, concat_axis=0,...]
    mul x8 -> x0, other arithmetic: 26.7 us -> none  [the longest x1 13.4 us: shards(): propagate(masked, extended[:, :, :-2], extended[:, :, 2:], speed_x, speed_y)]
    add x2 -> x0, other arithmetic: 21.5 us -> none  [the longest x1 20.9 us: turn_spectrum(): turned + weight_off[None] * padded[REACH + offset:REACH + offset + dir_co...]
  transfers between devices with their start and end apart: 5 -> 0, of which waited for: 5 -> 0; matrix products, arithmetic and copies ran while one was open for 1% -> 0% of each run, Pallas kernels for 0% -> 0%
where the time goes in v1:
time: 183 us
  Pallas kernels  175 us (96%)
  local copies, waits for them, and re-layouts  7.96 us (4%)
    pallas_call x1, Pallas kernels, shards(): pl.pallas_call(functools.partial(kernel, dir_groups, space_groups), out_s...  175 us
    unnamed x2, local copies, waits for them, and re-layouts  7.96 us

profile of v1, /device:TPU:0, one launch (start us, length us, event | category | flops | bytes accessed | tf_op | source)
XLA Modules:
  0.0 183.0 jit_solution(1656311119331510304)
XLA Ops:
  0.0 1.4 copy.15.shift_ref
  1.4 175.0 %wave_step.1 = f32[288,24,256]{2,1,0:T(8,128)} custom-call(f32[6912,256]{1,0:T(8,128)} %bitcast.4, s32[24,256]{1,0:T(8,128)} %land_ref.1, s32[24,256]{1,0:T(8,128)} %depth_ref.1, s32[24,8]{1,0:T(8,128)} %copy.15.shift_ref, f32[24,256]{1,0:T(8,128)} %turning_ref.1, f32[24,256]{1,0:T(8,128)} %rate_ref.1, f32[24,256]{1,0:T(8,128)} %wind_ref.1, f32[32]{0:T(128)} %cfl_ref.1, ...), custom_call_target="tpu_custom_call" | custom-call | tf_op jit(solution)/shard_map/wave_step/pallas_call | solution.py:403
  176.4 6.6 %copy.17 = f32[18,16,24,256]{3,2,1,0:T(8,128)} copy(f32[18,16,24,256]{3,2,1,0:T(8,128)} %bitcast.3) | data formatting | bytes 14155776

commit v2 on v1

--- a/solution.py
+++ b/solution.py
@@ -21,7 +21,7 @@
 def kernel(
     dir_groups,
     space_groups,
-    spec_ref,
+    spectrum_ref,
     land_ref,
     depth_ref,
     shift_ref,
@@ -36,12 +36,12 @@
     sigma_ref,
     transfer_ref,
     out_ref,
+    spec_ref,
     grid_buf,
     turned_buf,
     own_part,
     send_part,
     recv_part,
-    out_buf,
     matrix,
     raw_matrix,
     edge_top,
@@ -52,6 +52,7 @@
     shift_wide,
     coswind,
     sinwind,
+    spec_sem,
     matrix_sem,
     halo_send,
     halo_recv,
@@ -59,7 +60,6 @@
     dir_recv,
     part_send,
     part_recv,
-    out_sem,
 ):
     me_dir = lax.axis_index("dir")
     me_space = lax.axis_index("space")
@@ -93,6 +93,15 @@
     def _():
         pl.semaphore_signal(barrier, inc=1, device_id={"space": me_space + 1}, device_id_type=MESH_ID)
 
+    def spec_copy(d):
+        piece = pl.ds(pl.multiple_of(d * freq_local * row_count, ROWS), freq_local * row_count)
+        return pltpu.make_async_copy(spectrum_ref.at[piece], spec_ref.at[piece], spec_sem.at[d])
+
+    def start_copy(d, carry):
+        spec_copy(d).start()
+        return carry
+
+    lax.fori_loop(0, dir_local, start_copy, 0)
     matrix_copy = pltpu.make_async_copy(
         transfer_ref.at[:, pl.ds(freq_first, freq_local), :], raw_matrix, matrix_sem
     )
@@ -103,15 +112,12 @@
     first_sea = sea_ref[pl.ds(0, ROWS), :]
     last_sea = sea_ref[pl.ds(row_count - ROWS, ROWS), :]
 
-    def pack(b, carry):
+    def pack(b):
         base = pl.multiple_of(b * row_count, ROWS)
         top = spec_ref[pl.ds(base, ROWS), :] * first_sea
         low = spec_ref[pl.ds(base + row_count - ROWS, ROWS), :] * last_sea
         edge_top[pl.ds(b, 1), :] = top[:1]
         edge_bot[pl.ds(b, 1), :] = low[ROWS - 1 :]
-        return carry
-
-    lax.fori_loop(0, bins, pack, 0, unroll=8)
 
     pl.semaphore_wait(
         barrier,
@@ -137,16 +143,8 @@
         device_id_type=MESH_ID,
     )
 
-    @pl.when(me_space > 0)
-    def _():
-        up_copy.start()
-
-    @pl.when(me_space < space_groups - 1)
-    def _():
-        down_copy.start()
-
-    def dir_copy(c, j):
-        region = grid_buf.at[c, pl.ds(dir_first, dir_local)]
+    def dir_copy(c, j, first=0, count=dir_local):
+        region = grid_buf.at[c, pl.ds(dir_first + first, count)]
         return pltpu.make_async_remote_copy(
             src_ref=region,
             dst_ref=region,
@@ -167,11 +165,15 @@
             sea_next = sea_ref[pl.ds(tile * ROWS + ROWS, ROWS), :]
 
         def per_dir(d, carry):
+            if place == 0:
+                spec_copy(d).wait()
             cos_d = cos_ref[dir_first + d]
             sin_d = sin_ref[dir_first + d]
 
             def per_freq(f, inner):
                 b = d * freq_local + f
+                if place == 0:
+                    pack(b)
                 base = pl.multiple_of(b * row_count, ROWS)
                 here = spec_ref[pl.ds(base + tile * ROWS, ROWS), :] * sea
                 if tile > 0:
@@ -200,18 +202,32 @@
                     grid_buf[place * halves + h, dir_first + d, f] = moved[:, h * LANES : (h + 1) * LANES]
                 return inner
 
-            return lax.fori_loop(0, freq_local, per_freq, carry, unroll=4)
+            lax.fori_loop(0, freq_local, per_freq, 0, unroll=4)
+            if place == 0:
+                for h in range(halves):
+                    for j in range(1, dir_groups):
+                        dir_copy(h, j, d, 1).start()
+            return carry
 
         lax.fori_loop(0, dir_local, per_dir, 0)
-        for h in range(halves):
-            for j in range(1, dir_groups):
-                dir_copy(place * halves + h, j).start()
+        if place > 0:
+            for h in range(halves):
+                for j in range(1, dir_groups):
+                    dir_copy(place * halves + h, j).start()
 
     for place in range(tiles - 2):
         propagate(place + 1, place)
 
     @pl.when(me_space > 0)
     def _():
+        up_copy.start()
+
+    @pl.when(me_space < space_groups - 1)
+    def _():
+        down_copy.start()
+
+    @pl.when(me_space > 0)
+    def _():
         up_copy.wait_send()
         down_copy.wait_recv()
 
@@ -233,14 +249,16 @@
 
     coswind[...] = jnp.cos(wind_ref[...])
     sinwind[...] = jnp.sin(wind_ref[...])
-    table_cols = lax.broadcasted_iota(jnp.int32, (row_count, col_count), 1)
-    shift_tiles = shift_ref.shape[1]
+    shift_tiles = shift_ref.shape[0]
     width = col_count // shift_tiles
-    wide = jnp.zeros((row_count, col_count), jnp.int32)
-    for s in range(shift_tiles):
-        inside = (table_cols >= s * width) & (table_cols < (s + 1) * width)
-        wide = jnp.where(inside, jnp.broadcast_to(shift_ref[:, s : s + 1], wide.shape), wide)
-    shift_wide[...] = wide
+    tile_of = lax.broadcasted_iota(jnp.int32, (shift_tiles, col_count), 1) // width
+    tile_id = lax.broadcasted_iota(jnp.int32, (shift_tiles, col_count), 0)
+    shift_wide[...] = lax.dot_general(
+        shift_ref[...].astype(jnp.float32),
+        (tile_of == tile_id).astype(jnp.float32),
+        (((0,), (0,)), ((), ())),
+        preferred_element_type=jnp.float32,
+    ).astype(jnp.int32)
 
     matrix_copy.wait()
     depth = dir_total * freq_local
@@ -255,7 +273,11 @@
                 piece * freq_local : (piece + 1) * freq_local
             ]
 
+    middle = (dir_local + 1) // 2
+    piece_ends = ((0, middle), (middle, dir_local))
+
     def chunk(c, carry):
+        slot = c % 2
         place = c // halves
         half = c % halves
         tile = jnp.where(place < tiles - 2, place + 1, jnp.where(place == tiles - 2, 0, tiles - 1))
@@ -291,41 +313,49 @@
 
         zero = jnp.zeros((ROWS, LANES), jnp.float32)
         energy, moment = lax.fori_loop(0, freq_local, refract, (zero, zero))
-        send_part[pl.ds(bins * ROWS, ROWS), :] = energy
-        send_part[pl.ds((bins + 1) * ROWS, ROWS), :] = moment
-
-        mine = pl.ds(pl.multiple_of(dir_first * freq_local, 16), bins)
-
-        def mix(pair, inner):
-            first = turned_buf[pl.ds(2 * pair, depth, stride=ROWS), :]
-            second = turned_buf[pl.ds(2 * pair + 1, depth, stride=ROWS), :]
-            both = jnp.concatenate([first, second], axis=1)
-            high = both.astype(jnp.bfloat16)
-            low = (both - high.astype(jnp.float32)).astype(jnp.bfloat16)
-            right = jnp.concatenate([high, high, low], axis=0)
-            left = jnp.concatenate([matrix[me_freq, mine, :], matrix[other_freq, mine, :]], axis=0)
-            part = jnp.dot(left, right, preferred_element_type=jnp.float32)
-            own_part[pl.ds(2 * pair, bins, stride=ROWS), :] = part[:bins, :LANES]
-            own_part[pl.ds(2 * pair + 1, bins, stride=ROWS), :] = part[:bins, LANES:]
-            send_part[pl.ds(2 * pair, bins, stride=ROWS), :] = part[bins:, :LANES]
-            send_part[pl.ds(2 * pair + 1, bins, stride=ROWS), :] = part[bins:, LANES:]
-            return inner
-
-        lax.fori_loop(0, ROWS // 2, mix, 0)
-        swap = pltpu.make_async_remote_copy(
-            src_ref=send_part,
-            dst_ref=recv_part.at[c],
-            send_sem=part_send.at[c],
-            recv_sem=part_recv.at[c],
-            device_id={"freq": other_freq},
-            device_id_type=MESH_ID,
-        )
-        swap.start()
-        swap.wait()
+        send_part[pl.ds(0, ROWS), :] = energy
+        send_part[pl.ds(ROWS, ROWS), :] = moment
+
+        def swap(n):
+            first, last = piece_ends[n]
+            first = 0 if n == 0 else (first * freq_local + 2) * ROWS
+            piece = pl.ds(first, (last * freq_local + 2) * ROWS - first)
+            return pltpu.make_async_remote_copy(
+                src_ref=send_part.at[piece],
+                dst_ref=recv_part.at[slot, piece],
+                send_sem=part_send.at[slot, n],
+                recv_sem=part_recv.at[slot, n],
+                device_id={"freq": other_freq},
+                device_id_type=MESH_ID,
+            )
+
+        for n, (first_dir, last_dir) in enumerate(piece_ends):
+            size = (last_dir - first_dir) * freq_local
+            start = first_dir * freq_local * ROWS
+            mine = pl.ds(pl.multiple_of((dir_first + first_dir) * freq_local, 16), size)
+
+            def mix(pair, inner):
+                first = turned_buf[pl.ds(2 * pair, depth, stride=ROWS), :]
+                second = turned_buf[pl.ds(2 * pair + 1, depth, stride=ROWS), :]
+                both = jnp.concatenate([first, second], axis=1)
+                high = both.astype(jnp.bfloat16)
+                low = (both - high.astype(jnp.float32)).astype(jnp.bfloat16)
+                right = jnp.concatenate([high, high, low], axis=0)
+                left = jnp.concatenate([matrix[me_freq, mine, :], matrix[other_freq, mine, :]], axis=0)
+                part = jnp.dot(left, right, preferred_element_type=jnp.float32)
+                for k in range(2):
+                    lanes = slice(k * LANES, (k + 1) * LANES)
+                    own_part[pl.ds(start + 2 * pair + k, size, stride=ROWS), :] = part[:size, lanes]
+                    send_part[pl.ds(start + 2 * ROWS + 2 * pair + k, size, stride=ROWS), :] = part[size:, lanes]
+                return inner
+
+            lax.fori_loop(0, ROWS // 2, mix, 0)
+            swap(n).start()
+        swap(0).wait_recv()
 
         sea = sea_ref[rows, cols]
-        energy = (energy + recv_part[c, pl.ds(bins * ROWS, ROWS), :]) / bin_total
-        moment = (moment + recv_part[c, pl.ds((bins + 1) * ROWS, ROWS), :]) / bin_total
+        energy = (energy + recv_part[slot, pl.ds(0, ROWS), :]) / bin_total
+        moment = (moment + recv_part[slot, pl.ds(ROWS, ROWS), :]) / bin_total
         mean_sigma = moment / (energy + small_eps)
         steepness = energy * mean_sigma * mean_sigma
         white = whitecap_coef * (steepness * steepness)
@@ -335,36 +365,37 @@
         sin_w = sinwind[rows, cols]
         classes = depth_ref[rows, cols]
 
-        def source(f, inner):
-            sigma = sigma_ref[freq_first + f]
-            friction = jnp.full((ROWS, LANES), fric_ref[0, freq_first + f], jnp.float32)
-            for k in range(1, class_count):
-                friction = jnp.where(classes == k, fric_ref[k, freq_first + f], friction)
-            keep = sea * (1.0 - white * sigma - friction)
-            grow = rate * sigma
-            for d in range(dir_local):
-                at = pl.ds(pl.multiple_of((d * freq_local + f) * ROWS, ROWS), ROWS)
-                whole = pl.ds(pl.multiple_of(((dir_first + d) * freq_local + f) * ROWS, ROWS), ROWS)
-                align = jnp.maximum(cos_ref[dir_first + d] * cos_w + sin_ref[dir_first + d] * sin_w, 0.0)
-                mixed = own_part[at, :] + recv_part[c, at, :]
-                out_buf[c, d * freq_local + f] = (
-                    turned_buf[whole, :] * (keep + grow * align) + nonlinear * mixed
-                )
-            return inner
-
-        lax.fori_loop(0, freq_local, source, 0)
-        out_copy(c, rows, cols).start()
+        for n, (first_dir, last_dir) in enumerate(piece_ends):
+            if n > 0:
+                swap(n).wait_recv()
+
+            def source(f, inner):
+                sigma = sigma_ref[freq_first + f]
+                friction = jnp.full((ROWS, LANES), fric_ref[0, freq_first + f], jnp.float32)
+                for k in range(1, class_count):
+                    friction = jnp.where(classes == k, fric_ref[k, freq_first + f], friction)
+                keep = sea * (1.0 - white * sigma - friction)
+                grow = rate * sigma
+                for d in range(first_dir, last_dir):
+                    spot = d * freq_local + f
+                    at = pl.ds(pl.multiple_of(spot * ROWS, ROWS), ROWS)
+                    there = pl.ds(pl.multiple_of((spot + 2) * ROWS, ROWS), ROWS)
+                    whole = pl.ds(pl.multiple_of(((dir_first + d) * freq_local + f) * ROWS, ROWS), ROWS)
+                    align = jnp.maximum(cos_ref[dir_first + d] * cos_w + sin_ref[dir_first + d] * sin_w, 0.0)
+                    mixed = own_part[at, :] + recv_part[slot, there, :]
+                    out_ref[spot, rows, cols] = turned_buf[whole, :] * (keep + grow * align) + nonlinear * mixed
+                return inner
+
+            lax.fori_loop(0, freq_local, source, 0)
+        for n in range(len(piece_ends)):
+            swap(n).wait_send()
         return carry
-
-    def out_copy(c, rows, cols):
-        return pltpu.make_async_copy(out_buf.at[c], out_ref.at[:, rows, cols], out_sem.at[c])
 
     lax.fori_loop(0, chunks, chunk, 0)
 
     def finish(c, carry):
         for j in range(1, dir_groups):
             dir_copy(c, j).wait_send()
-        out_copy(c, pl.ds(0, ROWS), pl.ds(0, LANES)).wait()
         return carry
 
     lax.fori_loop(0, chunks, finish, 0)
@@ -402,16 +433,16 @@
     f32 = jnp.float32
     evolved = pl.pallas_call(
         functools.partial(kernel, dir_groups, space_groups),
-        out_shape=jax.ShapeDtypeStruct((bins, row_count, col_count), f32),
-        in_specs=[vmem] * 7 + [smem] * 6 + [anywhere],
-        out_specs=anywhere,
+        out_shape=pltpu.VMEM((bins, row_count, col_count), f32),
+        in_specs=[anywhere] + [vmem] * 6 + [smem] * 6 + [anywhere],
+        out_specs=vmem,
         scratch_shapes=[
+            pltpu.VMEM((bins * row_count, col_count), f32),
             pltpu.VMEM((chunks, dir_total, freq_local, ROWS, LANES), f32),
             pltpu.VMEM((depth * ROWS, LANES), f32),
             pltpu.VMEM((bins * ROWS, LANES), f32),
             pltpu.VMEM(((bins + 2) * ROWS, LANES), f32),
-            pltpu.VMEM((chunks, (bins + 2) * ROWS, LANES), f32),
-            pltpu.VMEM((chunks, bins, ROWS, LANES), f32),
+            pltpu.VMEM((2, (bins + 2) * ROWS, LANES), f32),
             pltpu.VMEM((2, depth, 3 * depth), jnp.bfloat16),
             pltpu.VMEM((dir_total, freq_local, transfer.shape[1]), f32),
             pltpu.VMEM((bins, col_count), f32),
@@ -422,24 +453,24 @@
             pltpu.VMEM((row_count, col_count), jnp.int32),
             pltpu.VMEM((row_count, col_count), f32),
             pltpu.VMEM((row_count, col_count), f32),
+            pltpu.SemaphoreType.DMA((dir_local,)),
             pltpu.SemaphoreType.DMA,
             pltpu.SemaphoreType.DMA((2,)),
             pltpu.SemaphoreType.DMA((2,)),
             pltpu.SemaphoreType.DMA((chunks, peers)),
             pltpu.SemaphoreType.DMA((chunks, peers)),
-            pltpu.SemaphoreType.DMA((chunks,)),
-            pltpu.SemaphoreType.DMA((chunks,)),
-            pltpu.SemaphoreType.DMA((chunks,)),
+            pltpu.SemaphoreType.DMA((2, 2)),
+            pltpu.SemaphoreType.DMA((2, 2)),
         ],
         compiler_params=pltpu.CompilerParams(
-            collective_id=0, has_side_effects=True, vmem_limit_bytes=60 * 1024 * 1024
+            collective_id=0, has_side_effects=True, vmem_limit_bytes=44 * 1024 * 1024
         ),
         name="wave_step",
     )(
         spectrum.reshape(bins * row_count, col_count),
         land_mask,
         depth_class,
-        shift_count,
+        shift_count.T,
         turning,
         wind_rate,
         wind_angle,

time: 183 us -> 177 us (0.967)
  Pallas kernels: 175 us -> 165 us
  local copies, waits for them, and re-layouts: 7.96 us -> 11.3 us
    pallas_call x1, Pallas kernels: 175 us -> 165 us  [shards(): pl.pallas_call(functools.partial(kernel, dir_groups, space_groups), out_s...]
    unnamed x2 -> x25, local copies, waits for them, and re-layouts: 7.96 us -> 11.3 us
where the time goes in v2:
time: 177 us; the launch traced here: 176 us
  Pallas kernels  165 us (93%)
  local copies, waits for them, and re-layouts  11.3 us (6%)
    pallas_call x1, Pallas kernels, shards(): pl.pallas_call(functools.partial(kernel, dir_groups, space_groups), out_s...  165 us
    unnamed x25, local copies, waits for them, and re-layouts  11.3 us

profile of v2, /device:TPU:0, one launch (start us, length us, event | category | flops | bytes accessed | tf_op | source)
XLA Modules:
  0.0 175.8 jit_solution(5760031023433491324)
XLA Ops:
  0.0 0.0 copy-start
  0.0 0.7 copy-done
  0.7 0.0 copy-start.1
  0.7 0.7 copy-done.1
  1.5 0.0 copy-start.2
  1.5 0.7 copy-done.2
  2.2 0.0 copy-start.3
  2.2 0.7 copy-done.3
  3.0 0.0 copy-start.4
  3.0 0.7 copy-done.4
  3.7 0.0 copy-start.5
  3.7 0.7 copy-done.5
  4.4 0.0 copy-start.6
  4.4 0.7 copy-done.6
  5.1 0.0 copy-start.7
  5.1 0.7 copy-done.7
  5.7 0.0 copy-start.8
  5.7 0.7 copy-done.8
  6.4 0.0 copy-start.9
  6.4 0.7 copy-done.9
  7.0 0.0 copy-start.10
  7.0 0.7 copy-done.10
  7.7 0.0 copy-start.11
  7.7 0.7 copy-done.11
  8.3 164.5 %wave_step.1 = f32[288,24,256]{2,1,0:T(8,128)S(1)} custom-call(f32[6912,256]{1,0:T(8,128)} %bitcast.6, s32[24,256]{1,0:T(8,128)S(1)} %copy-done, s32[24,256]{1,0:T(8,128)S(1)} %copy-done.1, s32[8,24]{1,0:T(8,128)S(1)} %bitcast.5, f32[24,256]{1,0:T(8,128)S(1)} %copy-done.2, f32[24,256]{1,0:T(8,128)S(1)} %copy-done.3, f32[24,256]{1,0:T(8,128)S(1)} %copy-done.4, ...), custom_call_target="tpu_custom_call" | custom-call | tf_op jit(solution)/shard_map/wave_step/pallas_call | solution.py:434
  172.9 3.0 %copy.16 = f32[18,16,24,256]{3,2,1,0:T(8,128)} copy(f32[18,16,24,256]{3,2,1,0:T(8,128)S(1)} %bitcast.4) | data formatting | bytes 14155776
Async XLA Ops:
  0.0 0.7 copy-start
  0.7 0.7 copy-start.1
  1.5 0.7 copy-start.2
  2.2 0.7 copy-start.3
  3.0 0.7 copy-start.4
  3.7 0.7 copy-start.5
  4.4 0.7 copy-start.6
  5.1 0.7 copy-start.7
  5.7 0.7 copy-start.8
  6.4 0.7 copy-start.9
  7.0 0.7 copy-start.10
  7.7 0.7 copy-start.11

commit v3 on v2

--- a/solution.py
+++ b/solution.py
@@ -22,6 +22,20 @@
     dir_groups,
     space_groups,
     spectrum_ref,
+    land_hbm,
+    depth_hbm,
+    shift_hbm,
+    turning_hbm,
+    rate_hbm,
+    wind_hbm,
+    cfl_hbm,
+    turn_hbm,
+    fric_hbm,
+    cos_hbm,
+    sin_hbm,
+    sigma_hbm,
+    transfer_ref,
+    out_ref,
     land_ref,
     depth_ref,
     shift_ref,
@@ -34,8 +48,7 @@
     cos_ref,
     sin_ref,
     sigma_ref,
-    transfer_ref,
-    out_ref,
+    small_sem,
     spec_ref,
     grid_buf,
     turned_buf,
@@ -93,6 +106,28 @@
     def _():
         pl.semaphore_signal(barrier, inc=1, device_id={"space": me_space + 1}, device_id_type=MESH_ID)
 
+    small = [
+        pltpu.make_async_copy(source, table, small_sem.at[n])
+        for n, (source, table) in enumerate(
+            (
+                (land_hbm, land_ref),
+                (cfl_hbm, cfl_ref),
+                (cos_hbm, cos_ref),
+                (sin_hbm, sin_ref),
+                (turning_hbm, turning_ref),
+                (turn_hbm, turn_ref),
+                (fric_hbm, fric_ref),
+                (sigma_hbm, sigma_ref),
+                (depth_hbm, depth_ref),
+                (shift_hbm, shift_ref),
+                (rate_hbm, rate_ref),
+                (wind_hbm, wind_ref),
+            )
+        )
+    ]
+    for copy in small:
+        copy.start()
+
     def spec_copy(d):
         piece = pl.ds(pl.multiple_of(d * freq_local * row_count, ROWS), freq_local * row_count)
         return pltpu.make_async_copy(spectrum_ref.at[piece], spec_ref.at[piece], spec_sem.at[d])
@@ -107,6 +142,8 @@
     )
     matrix_copy.start()
 
+    for copy in small[:4]:
+        copy.wait()
     sea_ref[...] = jnp.where(land_ref[...] == 1, 1.0, 0.0)
 
     first_sea = sea_ref[pl.ds(0, ROWS), :]
@@ -247,6 +284,8 @@
     propagate(0, tiles - 2)
     propagate(tiles - 1, tiles - 1)
 
+    for copy in small[4:]:
+        copy.wait()
     coswind[...] = jnp.cos(wind_ref[...])
     sinwind[...] = jnp.sin(wind_ref[...])
     shift_tiles = shift_ref.shape[0]
@@ -428,15 +467,30 @@
     depth = dir_total * freq_local
     peers = max(dir_groups - 1, 1)
     vmem = pl.BlockSpec(memory_space=pltpu.VMEM)
-    smem = pl.BlockSpec(memory_space=pltpu.SMEM)
-    anywhere = pl.BlockSpec(memory_space=pl.ANY)
+    hbm = pl.BlockSpec(memory_space=pltpu.HBM)
+    shift_tiles = shift_count.shape[1]
+    class_count = friction_table.shape[0]
+    points = (row_count, col_count)
     f32 = jnp.float32
     evolved = pl.pallas_call(
         functools.partial(kernel, dir_groups, space_groups),
         out_shape=pltpu.VMEM((bins, row_count, col_count), f32),
-        in_specs=[anywhere] + [vmem] * 6 + [smem] * 6 + [anywhere],
+        in_specs=[hbm] * 14,
         out_specs=vmem,
         scratch_shapes=[
+            pltpu.VMEM(points, jnp.int32),
+            pltpu.VMEM(points, jnp.int32),
+            pltpu.VMEM((shift_tiles, row_count), jnp.int32),
+            pltpu.VMEM(points, f32),
+            pltpu.VMEM(points, f32),
+            pltpu.VMEM(points, f32),
+            pltpu.SMEM((freq_total,), f32),
+            pltpu.SMEM((freq_total,), f32),
+            pltpu.SMEM((class_count, freq_total), f32),
+            pltpu.SMEM((dir_total,), f32),
+            pltpu.SMEM((dir_total,), f32),
+            pltpu.SMEM((freq_total,), f32),
+            pltpu.SemaphoreType.DMA((12,)),
             pltpu.VMEM((bins * row_count, col_count), f32),
             pltpu.VMEM((chunks, dir_total, freq_local, ROWS, LANES), f32),
             pltpu.VMEM((depth * ROWS, LANES), f32),
@@ -463,7 +517,7 @@
             pltpu.SemaphoreType.DMA((2, 2)),
         ],
         compiler_params=pltpu.CompilerParams(
-            collective_id=0, has_side_effects=True, vmem_limit_bytes=44 * 1024 * 1024
+            collective_id=0, has_side_effects=True, vmem_limit_bytes=52 * 1024 * 1024
         ),
         name="wave_step",
     )(

time: 177 us -> 168 us (0.949)
  local copies, waits for them, and re-layouts: 11.3 us -> 2.96 us
    unnamed x25 -> x1, local copies, waits for them, and re-layouts: 11.3 us -> 2.96 us
where the time goes in v3:
time: 168 us; the launch traced here: 167 us
  Pallas kernels  164 us (98%)
  local copies, waits for them, and re-layouts  2.96 us (2%)
    pallas_call x1, Pallas kernels, shards(): pl.pallas_call(functools.partial(kernel, dir_groups, space_groups), out_s...  164 us

profile of v3, /device:TPU:0, one launch (start us, length us, event | category | flops | bytes accessed | tf_op | source)
XLA Modules:
  0.0 166.9 jit_solution(2198632222432612487)
XLA Ops:
  0.0 164.0 %wave_step.1 = f32[288,24,256]{2,1,0:T(8,128)S(1)} custom-call(f32[6912,256]{1,0:T(8,128)} %bitcast.5, s32[24,256]{1,0:T(8,128)} %land_hbm.1, s32[24,256]{1,0:T(8,128)} %depth_hbm.1, s32[8,24]{1,0:T(8,128)} %bitcast.7, f32[24,256]{1,0:T(8,128)} %turning_hbm.1, f32[24,256]{1,0:T(8,128)} %rate_hbm.1, f32[24,256]{1,0:T(8,128)} %wind_hbm.1, f32[32]{0:T(128)} %cfl_hbm.1, ...), custom_call_target="tpu_custom_call" | custom-call | tf_op jit(solution)/shard_map/wave_step/pallas_call | solution.py:475
  164.0 3.0 %copy.16 = f32[18,16,24,256]{3,2,1,0:T(8,128)} copy(f32[18,16,24,256]{3,2,1,0:T(8,128)S(1)} %bitcast.4) | data formatting | bytes 14155776

commit v4 on v3

--- a/solution.py
+++ b/solution.py
@@ -11,6 +11,7 @@
 
 ROWS = 8
 LANES = 128
+TAIL = 4
 MESH_ID = pl.DeviceIdType.MESH
 
 whitecap_coef = 0.01
@@ -57,6 +58,10 @@
     recv_part,
     matrix,
     raw_matrix,
+    raw_other,
+    tail_matrix,
+    tail_send,
+    tail_recv,
     edge_top,
     edge_bot,
     halo_up,
@@ -67,6 +72,9 @@
     sinwind,
     spec_sem,
     matrix_sem,
+    other_sem,
+    tail_send_sem,
+    tail_recv_sem,
     halo_send,
     halo_recv,
     dir_send,
@@ -141,6 +149,12 @@
         transfer_ref.at[:, pl.ds(freq_first, freq_local), :], raw_matrix, matrix_sem
     )
     matrix_copy.start()
+    other_copy = pltpu.make_async_copy(
+        transfer_ref.at[:, pl.ds(pl.multiple_of(other_freq * freq_local + freq_local - ROWS, ROWS), ROWS), :],
+        raw_other,
+        other_sem,
+    )
+    other_copy.start()
 
     for copy in small[:4]:
         copy.wait()
@@ -180,16 +194,24 @@
         device_id_type=MESH_ID,
     )
 
-    def dir_copy(c, j, first=0, count=dir_local):
-        region = grid_buf.at[c, pl.ds(dir_first + first, count)]
+    head = freq_local - TAIL
+
+    def dir_copy(c, j, first=0, count=dir_local, low=0, bands=freq_local, sem=None):
+        sem = c if sem is None else sem
+        region = grid_buf.at[c, pl.ds(dir_first + first, count), pl.ds(low, bands)]
         return pltpu.make_async_remote_copy(
             src_ref=region,
             dst_ref=region,
-            send_sem=dir_send.at[c, j - 1],
-            recv_sem=dir_recv.at[c, j - 1],
+            send_sem=dir_send.at[sem, j - 1],
+            recv_sem=dir_recv.at[sem, j - 1],
             device_id={"dir": lax.rem(me_dir + j, dir_groups)},
             device_id_type=MESH_ID,
         )
+
+    def last_copy(j, n):
+        if n == 0:
+            return dir_copy(chunks - 1, j, low=0, bands=head)
+        return dir_copy(chunks - 1, j, low=head, bands=TAIL, sem=chunks)
 
     row_id = lax.broadcasted_iota(jnp.int32, (ROWS, col_count), 0)
     col_id = lax.broadcasted_iota(jnp.int32, (ROWS, col_count), 1)
@@ -250,7 +272,11 @@
         if place > 0:
             for h in range(halves):
                 for j in range(1, dir_groups):
-                    dir_copy(place * halves + h, j).start()
+                    if place * halves + h == chunks - 1:
+                        for n in range(2):
+                            last_copy(j, n).start()
+                    else:
+                        dir_copy(place * halves + h, j).start()
 
     for place in range(tiles - 2):
         propagate(place + 1, place)
@@ -300,6 +326,7 @@
     ).astype(jnp.int32)
 
     matrix_copy.wait()
+    other_copy.wait()
     depth = dir_total * freq_local
     for m in range(bin_total // LANES):
         block = raw_matrix[:, :, m * LANES : (m + 1) * LANES].reshape(depth, LANES)
@@ -315,21 +342,42 @@
     middle = (dir_local + 1) // 2
     piece_ends = ((0, middle), (middle, dir_local))
 
-    def chunk(c, carry):
+    eight = lax.broadcasted_iota(jnp.int32, (dir_total // 2, ROWS, LANES), 1)
+    for m in range(bin_total // LANES):
+        lanes = slice(m * LANES, (m + 1) * LANES)
+        for side in range(2):
+            block = raw_other[:, :, lanes] if side else raw_matrix[:, freq_local - ROWS :, lanes]
+            pairs = block.reshape(dir_total // 2, 2, ROWS, LANES)
+            block = jnp.where(eight < TAIL, pltpu.roll(pairs[:, 0], TAIL, 1), pairs[:, 1])
+            block = block.reshape(dir_total * TAIL, LANES)
+            high = block.astype(jnp.bfloat16).astype(jnp.float32)
+            low = block - high
+            turned_block = jnp.concatenate([high, low, high], axis=0).T.astype(jnp.bfloat16)
+            for piece in range(LANES // freq_local):
+                d, g = divmod(m * (LANES // freq_local) + piece, 2)
+                tail_matrix[side, g, pl.ds(d * freq_local, freq_local), :] = turned_block[
+                    piece * freq_local : (piece + 1) * freq_local
+                ]
+
+    def chunk(c, last):
         slot = c % 2
-        place = c // halves
-        half = c % halves
-        tile = jnp.where(place < tiles - 2, place + 1, jnp.where(place == tiles - 2, 0, tiles - 1))
-        rows = pl.ds(pl.multiple_of(tile * ROWS, ROWS), ROWS)
-        cols = pl.ds(pl.multiple_of(half * LANES, LANES), LANES)
+        if last:
+            tile, half = tiles - 1, halves - 1
+        else:
+            place = c // halves
+            half = c % halves
+            tile = jnp.where(place < tiles - 2, place + 1, jnp.where(place == tiles - 2, 0, tiles - 1))
+        rows = pl.ds(tile * ROWS if last else pl.multiple_of(tile * ROWS, ROWS), ROWS)
+        cols = pl.ds(half * LANES if last else pl.multiple_of(half * LANES, LANES), LANES)
         for j in range(1, dir_groups):
-            dir_copy(c, j).wait_recv()
+            copy = last_copy(j, 0) if last else dir_copy(c, j)
+            copy.wait_recv()
 
         shift = shift_wide[rows, cols]
         turning = turning_ref[rows, cols]
         picks = [shift == k for k in range(-2, 2)]
 
-        def refract(f, sums):
+        def refract(in_tail, f, sums):
             weight = turning * turn_ref[freq_first + f]
             rest = 1.0 - weight
             moved = [grid_buf[c, d, f] for d in range(dir_total)]
@@ -346,12 +394,25 @@
                 now = shifted(d)
                 turned = rest * now + weight * before
                 turned_buf[pl.ds(pl.multiple_of((d * freq_local + f) * ROWS, ROWS), ROWS), :] = turned
+                if in_tail:
+                    spot = (d * TAIL + f - head + 2) * ROWS
+                    tail_send[pl.ds(pl.multiple_of(spot, ROWS), ROWS), :] = turned
                 total = total + turned
                 before = now
             return sums[0] + total, sums[1] + total * sigma_ref[freq_first + f]
 
         zero = jnp.zeros((ROWS, LANES), jnp.float32)
-        energy, moment = lax.fori_loop(0, freq_local, refract, (zero, zero))
+        energy, moment = lax.fori_loop(
+            0, head if last else freq_local, functools.partial(refract, False), (zero, zero)
+        )
+        if last:
+
+            def clear(d, inner):
+                spot = pl.multiple_of((d * freq_local + head) * ROWS, ROWS)
+                turned_buf[pl.ds(spot, TAIL * ROWS), :] = jnp.zeros((TAIL * ROWS, LANES), jnp.float32)
+                return inner
+
+            lax.fori_loop(0, dir_total, clear, 0)
         send_part[pl.ds(0, ROWS), :] = energy
         send_part[pl.ds(ROWS, ROWS), :] = moment
 
@@ -392,9 +453,54 @@
             swap(n).start()
         swap(0).wait_recv()
 
+        other_energy = recv_part[slot, pl.ds(0, ROWS), :]
+        other_moment = recv_part[slot, pl.ds(ROWS, ROWS), :]
+        if last:
+            swap(1).wait_recv()
+            for j in range(1, dir_groups):
+                last_copy(j, 1).wait_recv()
+            energy, moment = lax.fori_loop(
+                head, freq_local, functools.partial(refract, True), (energy, moment)
+            )
+            tail_send[pl.ds(0, ROWS), :] = energy
+            tail_send[pl.ds(ROWS, ROWS), :] = moment
+            tail_swap = pltpu.make_async_remote_copy(
+                src_ref=tail_send,
+                dst_ref=tail_recv,
+                send_sem=tail_send_sem,
+                recv_sem=tail_recv_sem,
+                device_id={"freq": other_freq},
+                device_id_type=MESH_ID,
+            )
+            tail_swap.start()
+            tail_rows = dir_total * TAIL
+            ours = pl.ds(pl.multiple_of(dir_first * freq_local, 16), bins)
+            for side, held in enumerate((tail_send, tail_recv)):
+                if side:
+                    tail_swap.wait_recv()
+
+                def mix_tail(pair, inner):
+                    first = held[pl.ds(2 * ROWS + 2 * pair, tail_rows, stride=ROWS), :]
+                    second = held[pl.ds(2 * ROWS + 2 * pair + 1, tail_rows, stride=ROWS), :]
+                    both = jnp.concatenate([first, second], axis=1)
+                    high = both.astype(jnp.bfloat16)
+                    low = (both - high.astype(jnp.float32)).astype(jnp.bfloat16)
+                    right = jnp.concatenate([high, high, low], axis=0)
+                    left = tail_matrix[side, me_freq, ours, :]
+                    part = jnp.dot(left, right, preferred_element_type=jnp.float32)
+                    for k in range(2):
+                        at = pl.ds(2 * pair + k, bins, stride=ROWS)
+                        own_part[at, :] = own_part[at, :] + part[:, k * LANES : (k + 1) * LANES]
+                    return inner
+
+                lax.fori_loop(0, ROWS // 2, mix_tail, 0)
+            other_energy = tail_recv[pl.ds(0, ROWS), :]
+            other_moment = tail_recv[pl.ds(ROWS, ROWS), :]
+            tail_swap.wait_send()
+
         sea = sea_ref[rows, cols]
-        energy = (energy + recv_part[slot, pl.ds(0, ROWS), :]) / bin_total
-        moment = (moment + recv_part[slot, pl.ds(ROWS, ROWS), :]) / bin_total
+        energy = (energy + other_energy) / bin_total
+        moment = (moment + other_moment) / bin_total
         mean_sigma = moment / (energy + small_eps)
         steepness = energy * mean_sigma * mean_sigma
         white = whitecap_coef * (steepness * steepness)
@@ -405,7 +511,7 @@
         classes = depth_ref[rows, cols]
 
         for n, (first_dir, last_dir) in enumerate(piece_ends):
-            if n > 0:
+            if n > 0 and not last:
                 swap(n).wait_recv()
 
             def source(f, inner):
@@ -428,16 +534,23 @@
             lax.fori_loop(0, freq_local, source, 0)
         for n in range(len(piece_ends)):
             swap(n).wait_send()
+
+    def run(c, carry):
+        chunk(c, False)
         return carry
 
-    lax.fori_loop(0, chunks, chunk, 0)
+    lax.fori_loop(0, chunks - 1, run, 0)
+    chunk(chunks - 1, True)
 
     def finish(c, carry):
         for j in range(1, dir_groups):
             dir_copy(c, j).wait_send()
         return carry
 
-    lax.fori_loop(0, chunks, finish, 0)
+    lax.fori_loop(0, chunks - 1, finish, 0)
+    for j in range(1, dir_groups):
+        for n in range(2):
+            last_copy(j, n).wait_send()
 
 
 def shards(
@@ -499,6 +612,10 @@
             pltpu.VMEM((2, (bins + 2) * ROWS, LANES), f32),
             pltpu.VMEM((2, depth, 3 * depth), jnp.bfloat16),
             pltpu.VMEM((dir_total, freq_local, transfer.shape[1]), f32),
+            pltpu.VMEM((dir_total, ROWS, transfer.shape[1]), f32),
+            pltpu.VMEM((2, 2, depth, 3 * dir_total * TAIL), jnp.bfloat16),
+            pltpu.VMEM(((dir_total * TAIL + 2) * ROWS, LANES), f32),
+            pltpu.VMEM(((dir_total * TAIL + 2) * ROWS, LANES), f32),
             pltpu.VMEM((bins, col_count), f32),
             pltpu.VMEM((bins, col_count), f32),
             pltpu.VMEM((bins, col_count), f32),
@@ -509,10 +626,13 @@
             pltpu.VMEM((row_count, col_count), f32),
             pltpu.SemaphoreType.DMA((dir_local,)),
             pltpu.SemaphoreType.DMA,
+            pltpu.SemaphoreType.DMA,
+            pltpu.SemaphoreType.DMA,
+            pltpu.SemaphoreType.DMA,
             pltpu.SemaphoreType.DMA((2,)),
             pltpu.SemaphoreType.DMA((2,)),
-            pltpu.SemaphoreType.DMA((chunks, peers)),
-            pltpu.SemaphoreType.DMA((chunks, peers)),
+            pltpu.SemaphoreType.DMA((chunks + 1, peers)),
+            pltpu.SemaphoreType.DMA((chunks + 1, peers)),
             pltpu.SemaphoreType.DMA((2, 2)),
             pltpu.SemaphoreType.DMA((2, 2)),
         ],

time: 168 us -> 166 us (0.988)
  no operation moved by 1% of the time
where the time goes in v4:
time: 166 us
  Pallas kernels  163 us (98%)
  local copies, waits for them, and re-layouts  2.96 us (2%)
    pallas_call x1, Pallas kernels, shards(): pl.pallas_call(functools.partial(kernel, dir_groups, space_groups), out_s...  163 us

profile of v4, /device:TPU:0, one launch (start us, length us, event | category | flops | bytes accessed | tf_op | source)
XLA Modules:
  0.0 166.1 jit_solution(6667359463284559602)
XLA Ops:
  0.0 163.1 %wave_step.1 = f32[288,24,256]{2,1,0:T(8,128)S(1)} custom-call(f32[6912,256]{1,0:T(8,128)} %bitcast.5, s32[24,256]{1,0:T(8,128)} %land_hbm.1, s32[24,256]{1,0:T(8,128)} %depth_hbm.1, s32[8,24]{1,0:T(8,128)} %bitcast.7, f32[24,256]{1,0:T(8,128)} %turning_hbm.1, f32[24,256]{1,0:T(8,128)} %rate_hbm.1, f32[24,256]{1,0:T(8,128)} %wind_hbm.1, f32[32]{0:T(128)} %cfl_hbm.1, ...), custom_call_target="tpu_custom_call" | custom-call | tf_op jit(solution)/shard_map/wave_step/pallas_call | solution.py:588
  163.1 3.0 %copy.16 = f32[18,16,24,256]{3,2,1,0:T(8,128)} copy(f32[18,16,24,256]{3,2,1,0:T(8,128)S(1)} %bitcast.4) | data formatting | bytes 14155776

commit v5 on v4

--- a/solution.py
+++ b/solution.py
@@ -361,6 +361,7 @@
 
     def chunk(c, last):
         slot = c % 2
+        pieces = ((0, dir_local),) if last else piece_ends
         if last:
             tile, half = tiles - 1, halves - 1
         else:
@@ -417,9 +418,9 @@
         send_part[pl.ds(ROWS, ROWS), :] = moment
 
         def swap(n):
-            first, last = piece_ends[n]
-            first = 0 if n == 0 else (first * freq_local + 2) * ROWS
-            piece = pl.ds(first, (last * freq_local + 2) * ROWS - first)
+            low, high = pieces[n]
+            low = 0 if n == 0 else (low * freq_local + 2) * ROWS
+            piece = pl.ds(low, (high * freq_local + 2) * ROWS - low)
             return pltpu.make_async_remote_copy(
                 src_ref=send_part.at[piece],
                 dst_ref=recv_part.at[slot, piece],
@@ -429,7 +430,7 @@
                 device_id_type=MESH_ID,
             )
 
-        for n, (first_dir, last_dir) in enumerate(piece_ends):
+        for n, (first_dir, last_dir) in enumerate(pieces):
             size = (last_dir - first_dir) * freq_local
             start = first_dir * freq_local * ROWS
             mine = pl.ds(pl.multiple_of((dir_first + first_dir) * freq_local, 16), size)
@@ -451,12 +452,7 @@
 
             lax.fori_loop(0, ROWS // 2, mix, 0)
             swap(n).start()
-        swap(0).wait_recv()
-
-        other_energy = recv_part[slot, pl.ds(0, ROWS), :]
-        other_moment = recv_part[slot, pl.ds(ROWS, ROWS), :]
         if last:
-            swap(1).wait_recv()
             for j in range(1, dir_groups):
                 last_copy(j, 1).wait_recv()
             energy, moment = lax.fori_loop(
@@ -493,10 +489,15 @@
                         own_part[at, :] = own_part[at, :] + part[:, k * LANES : (k + 1) * LANES]
                     return inner
 
-                lax.fori_loop(0, ROWS // 2, mix_tail, 0)
+                lax.fori_loop(0, ROWS // 2, mix_tail, 0, unroll=True)
             other_energy = tail_recv[pl.ds(0, ROWS), :]
             other_moment = tail_recv[pl.ds(ROWS, ROWS), :]
             tail_swap.wait_send()
+            swap(0).wait_recv()
+        else:
+            swap(0).wait_recv()
+            other_energy = recv_part[slot, pl.ds(0, ROWS), :]
+            other_moment = recv_part[slot, pl.ds(ROWS, ROWS), :]
 
         sea = sea_ref[rows, cols]
         energy = (energy + other_energy) / bin_total
@@ -510,8 +511,8 @@
         sin_w = sinwind[rows, cols]
         classes = depth_ref[rows, cols]
 
-        for n, (first_dir, last_dir) in enumerate(piece_ends):
-            if n > 0 and not last:
+        for n, (first_dir, last_dir) in enumerate(pieces):
+            if n > 0:
                 swap(n).wait_recv()
 
             def source(f, inner):
@@ -532,7 +533,7 @@
                 return inner
 
             lax.fori_loop(0, freq_local, source, 0)
-        for n in range(len(piece_ends)):
+        for n in range(len(pieces)):
             swap(n).wait_send()
 
     def run(c, carry):

time: 166 us -> 164 us (0.988)
  Pallas kernels: 163 us -> 160 us
    pallas_call x1, Pallas kernels: 163 us -> 160 us  [shards(): pl.pallas_call(functools.partial(kernel, dir_groups, space_groups), out_s...]
where the time goes in v5:
time: 164 us; the launch traced here: 163 us
  Pallas kernels  160 us (98%)
  local copies, waits for them, and re-layouts  2.96 us (2%)
    pallas_call x1, Pallas kernels, shards(): pl.pallas_call(functools.partial(kernel, dir_groups, space_groups), out_s...  160 us

profile of v5, /device:TPU:0, one launch (start us, length us, event | category | flops | bytes accessed | tf_op | source)
XLA Modules:
  0.0 163.3 jit_solution(9428099043223577872)
XLA Ops:
  0.0 160.4 %wave_step.1 = f32[288,24,256]{2,1,0:T(8,128)S(1)} custom-call(f32[6912,256]{1,0:T(8,128)} %bitcast.5, s32[24,256]{1,0:T(8,128)} %land_hbm.1, s32[24,256]{1,0:T(8,128)} %depth_hbm.1, s32[8,24]{1,0:T(8,128)} %bitcast.7, f32[24,256]{1,0:T(8,128)} %turning_hbm.1, f32[24,256]{1,0:T(8,128)} %rate_hbm.1, f32[24,256]{1,0:T(8,128)} %wind_hbm.1, f32[32]{0:T(128)} %cfl_hbm.1, ...), custom_call_target="tpu_custom_call" | custom-call | tf_op jit(solution)/shard_map/wave_step/pallas_call | solution.py:589
  160.4 3.0 %copy.16 = f32[18,16,24,256]{3,2,1,0:T(8,128)} copy(f32[18,16,24,256]{3,2,1,0:T(8,128)S(1)} %bitcast.4) | data formatting | bytes 14155776
